TPU v7x, 32 devices: a whole 2x2x4 slice. The times are simulated.
32 devices in a mesh: graph: 16 (over z, y, x), rep: 2 (over core).
Axes of the slice: x: 2, y: 2, z: 4, core: 2. Of those that a mesh axis runs over, the one named last changes fastest.
Arguments:
- grad_out: bfloat16 [8192, 256], P(('graph', 'rep')), may hold values from -6 to 6
- pre_act: bfloat16 [8192, 256], P(('graph', 'rep')), may hold values from -6 to 6
- aggregated: bfloat16 [8192, 256], P(('graph', 'rep')), may hold values from -0.3125 to 0.3125
- weight: bfloat16 [256, 256], replicated, may hold values from -0.375 to 0.375
- adj_tiles: bfloat16 [16, 2, 16, 2, 128, 128], P('graph', 'rep'), may hold values from 0 to 0.039794922
- tile_row: int32 [16, 2, 16, 2], P('graph', 'rep'), may hold values from 0 to 1
- tile_col: int32 [16, 2, 16, 2], P('graph', 'rep'), may hold values from 0 to 3
- tile_count: int32 [16, 2, 16], P('graph', 'rep'), may hold values from 0 to 2, as said below
- node_perm: int32 [16, 512], P('graph'), may hold values from 0 to 511, each once within a row
Outputs:
- input_grad: bfloat16 [8192, 256], P(('graph', 'rep'))
- weight_grad: float32 [256, 256], replicated
- relu_grad: bfloat16 [8192, 256], P(('graph', 'rep'))
Inputs may be any that keep to these rules, and one draw needn't show every extreme that they name: tile_count[g, r, g] is 2 for every partition g and replica r. `node_perm`: each row is a permutation.
All inputs are finite; a program needn't handle non-finite values.
Results may differ from a plain program's by a relative error of at most 0.0049.
Values may be sent and summed in bfloat16 or wider, within the bound.
A program may use at most 128 MiB of HBM per device.

v0:
```python
import jax
import jax.numpy as jnp
from jax import lax
from jax.sharding import PartitionSpec as P


def tile_products(running, sources, row_count, local_tiles, local_row, local_col, local_count):
    piece_parts = sources.shape[0] // row_count
    tile_size = local_tiles.shape[-1]
    feature_width = sources.shape[1]
    blocks = sources.reshape(piece_parts, row_count // tile_size, tile_size, feature_width)
    part_index = jnp.arange(piece_parts, dtype=jnp.int32)
    for slot_index in range(local_tiles.shape[1]):
        chosen = blocks[part_index, local_row[:, slot_index]]
        product = jnp.einsum(
            "kab,kac->kbc", local_tiles[:, slot_index], chosen, preferred_element_type=jnp.float32
        )
        alive = (local_count > slot_index).astype(jnp.float32)
        running = running.at[local_col[:, slot_index]].add(product * alive[:, None, None])
    return running


def body(
    grad_out, pre_act, aggregated, weight, adj_tiles, tile_row, tile_col, tile_count, node_perm
):
    row_count = grad_out.shape[0]
    feature_width = weight.shape[0]
    relu_grad = jnp.where(pre_act > 0, grad_out, jnp.zeros_like(grad_out))
    partial_weight = lax.dot_general(
        aggregated, relu_grad, (((0,), (0,)), ((), ())), preferred_element_type=jnp.float32
    )
    local_tiles = adj_tiles[0, 0]
    local_row = tile_row[0, 0]
    local_col = tile_col[0, 0]
    local_count = tile_count[0, 0]
    local_perm = node_perm[0]
    tile_size = local_tiles.shape[-1]
    col_blocks = lax.axis_size("rep") * (row_count // tile_size)
    empty = jnp.zeros((col_blocks, tile_size, feature_width), jnp.float32)
    back_agg = lax.dot_general(
        relu_grad, weight, (((1,), (1,)), ((), ())), preferred_element_type=jnp.float32
    ).astype(jnp.bfloat16)
    running = tile_products(
        empty,
        lax.all_gather(back_agg, "graph", axis=0, tiled=True),
        row_count,
        local_tiles,
        local_row,
        local_col,
        local_count,
    )
    partial_grad = running.reshape(col_blocks * tile_size, feature_width)
    input_grad = lax.psum_scatter(
        jnp.take(partial_grad, local_perm, axis=0), "rep", scatter_dimension=0, tiled=True
    ).astype(jnp.bfloat16)
    weight_grad = lax.psum(partial_weight, ("graph", "rep"))
    return (input_grad, weight_grad, relu_grad)


def solution(mesh):
    placed = (
        P(("graph", "rep"), None),
        P(("graph", "rep"), None),
        P(("graph", "rep"), None),
        P(),
        P("graph", "rep", None, None, None, None),
        P("graph", "rep", None, None),
        P("graph", "rep", None, None),
        P("graph", "rep", None),
        P("graph", None),
    )
    return jax.shard_map(
        body,
        mesh=mesh,
        in_specs=placed,
        out_specs=(P(("graph", "rep"), None), P(), P(("graph", "rep"), None)),
        check_vma=False,
    )
```

profile of v0, /device:TPU:0, one launch (start us, length us, event | category | flops | bytes accessed | tf_op | source)
XLA Modules:
  0.0 160.9 jit_solution(16786216906860122379)
XLA Ops:
  8.0 0.0 copy-start
  8.0 0.0 copy-start.2
  8.0 0.0 all-gather.2.cloned.1.call-start
  8.1 1.1 compare_select_fusion
  9.1 0.0 copy-done
  9.2 0.0 copy-start.1
  9.2 0.9 convolution_convert_fusion
  10.0 0.0 all-gather.2.cloned.1.call-update
  10.1 0.0 all-reduce.2.cloned.1.call-start
  10.1 1.8 %convolution_bitcast_fusion = f32[256,256]{0,1:T(8,128)} fusion(bf16[256,256]{1,0:T(8,128)(2,1)S(1)} %compare_select_fusion, bf16[256,256]{1,0:T(8,128)(2,1)} %param.11), kind=kOutput, calls=%fused_computation.7 | convolution fusion | flops 33554432 | bytes 524288 | tf_op jit(solution)/shard_map/dot_general | solution.py:29
  12.0 0.0 all-reduce.2.cloned.1.call-update
  12.0 0.0 reduce-scatter.2.cloned.1.call-start
  12.0 0.7 compare_select_fusion.1
  12.7 0.7 compare_and_fusion
  13.4 0.8 fusion.10
  14.2 0.8 fusion.6
  14.9 0.7 fusion.1
  15.6 0.0 copy-done.2
  15.6 0.1 copy.25
  15.7 60.0 %all-gather.2.cloned.1.call-done = bf16[4096,256]{1,0:T(8,128)(2,1)} async-done(((bf16[256,256]{1,0:T(8,128)(2,1)}), bf16[4096,256]{1,0:T(8,128)(2,1)}) %all-gather.2.cloned.1.call-update) | async-done | bytes 2097168 | tf_op jit(solution)/shard_map/all_gather | solution.py:45
  75.7 3.2 %gather_fusion.1 = bf16[16,128,256]{2,1,0:T(8,128)(2,1)} fusion(bf16[16,2,128,256]{3,2,1,0:T(8,128)(2,1)} %bitcast.44, s32[16]{0:T(128)S(1)} %get-tuple-element.9), kind=kCustom, calls=%fused_computation.1 | custom fusion | bytes 2097280 | tf_op jit(solution)/shard_map/gather | solution.py:14
  78.9 0.0 copy-done.1
  78.9 2.2 %gather_fusion = bf16[16,128,256]{2,1,0:T(8,128)(2,1)S(1)} fusion(bf16[16,2,128,256]{3,2,1,0:T(8,128)(2,1)} %bitcast.45, s32[16]{0:T(128)S(1)} %get-tuple-element.10), kind=kCustom, calls=%fused_computation | custom fusion | bytes 2097280 | tf_op jit(solution)/shard_map/gather | solution.py:14
  81.1 1.8 %multiply_bitcast_fusion.1 = f32[16,128,256]{1,2,0:T(8,128)} fusion(bf16[16,128,256]{2,1,0:T(8,128)(2,1)S(1)} %gather_fusion, f32[16]{0:T(128)S(1)} %get-tuple-element.14, bf16[16,2,128,128]{3,2,0,1:T(8,128)(2,1)S(1)} %bitcast.42), kind=kOutput, calls=%fused_computation.6 | convolution fusion | flops 134742016 | bytes 3670528 | tf_op jit(solution)/shard_map/kab,kac->kbc/dot_general | solution.py:15
  83.0 1.9 %copy.18 = f32[16,128,256]{2,1,0:T(8,128)S(1)} copy(f32[16,128,256]{1,2,0:T(8,128)} %multiply_bitcast_fusion.1) | data formatting | bytes 4194304 | tf_op jit(solution)/shard_map/mul | solution.py:19
  84.9 3.1 %multiply_bitcast_fusion = f32[16,128,256]{1,2,0:T(8,128)} fusion(bf16[16,128,256]{2,1,0:T(8,128)(2,1)} %gather_fusion.1, f32[16]{0:T(128)S(1)} %get-tuple-element.13, bf16[16,2,128,128]{3,2,0,1:T(8,128)(2,1)S(1)} %bitcast.43), kind=kOutput, calls=%fused_computation.5 | convolution fusion | flops 134742016 | bytes 3670528 | tf_op jit(solution)/shard_map/kab,kac->kbc/dot_general | solution.py:15
  88.0 2.9 %copy.20 = f32[16,128,256]{2,1,0:T(8,128)} copy(f32[16,128,256]{1,2,0:T(8,128)} %multiply_bitcast_fusion) | data formatting | bytes 4194304 | tf_op jit(solution)/shard_map/mul | solution.py:19
  90.9 2.2 %scatter_fusion = f32[4,128,256]{2,1,0:T(8,128)S(1)} fusion(f32[4,128,256]{2,1,0:T(8,128)S(1)} %broadcast_in_dim.10, s32[16]{0:T(128)S(1)} %get-tuple-element.12, f32[16,128,256]{2,1,0:T(8,128)S(1)} %copy.18), kind=kCustom, calls=%fused_computation.3 | custom fusion | flops 524288 | bytes 6291520 | tf_op jit(solution)/shard_map/scatter-add | solution.py:19
  93.1 3.5 %scatter_fusion.1 = f32[4,128,256]{2,1,0:T(8,128)S(1)} fusion(f32[4,128,256]{2,1,0:T(8,128)S(1)} %scatter_fusion, s32[16]{0:T(128)S(1)} %get-tuple-element.11, f32[16,128,256]{2,1,0:T(8,128)} %copy.20), kind=kCustom, calls=%fused_computation.4 | custom fusion | flops 524288 | bytes 6291520 | tf_op jit(solution)/shard_map/scatter-add | solution.py:19
  96.6 1.6 gather_fusion.2
  98.2 0.9 broadcast_select_fusion
  99.1 0.0 reduce-scatter.2.cloned.1.call-update
  99.1 51.0 %all-reduce.2.cloned.1.call-done = f32[256,256]{0,1:T(8,128)} async-done(((f32[256,256]{0,1:T(8,128)}), f32[256,256]{0,1:T(8,128)}) %all-reduce.2.cloned.1.call-update) | async-done | bytes 262160 | tf_op jit(solution)/shard_map/psum | solution.py:56
  150.1 1.8 %copy.21 = f32[256,256]{1,0:T(8,128)} copy(f32[256,256]{0,1:T(8,128)} %all-reduce.2.cloned.1.call-done) | data formatting | bytes 524288
  151.9 0.0 reduce-scatter.2.cloned.1.call-done
  151.9 1.6 %convert_element_type.31 = bf16[256,256]{1,0:T(8,128)(2,1)} convert(f32[256,256]{1,0:T(8,128)} %reduce-scatter.2.cloned.1.call-done) | non-fusion elementwise | flops 65536 | bytes 393216 | tf_op jit(solution)/shard_map/convert_element_type | solution.py:55
  (2 shorter events, 0.0 us)
Async XLA Ops:
  8.0 1.1 copy-start
  8.0 7.6 %copy-start.2 = (bf16[1,1,16,2,128,128]{5,4,3,2,1,0:T(8,128)(2,1)S(1)}, bf16[1,1,16,2,128,128]{5,4,3,2,1,0:T(8,128)(2,1)}, u32[]{:S(2)}) copy-start(bf16[1,1,16,2,128,128]{5,4,3,2,1,0:T(8,128)(2,1)} %param.13) | copy-start | bytes 3145732
  8.0 67.7 %all-gather.2.cloned.1.call-start = ((), (), s32[]{:S(2)}) async-start(), calls=%async_computation.1 | async-start | bytes 2228224 | tf_op jit(solution)/shard_map/all_gather | solution.py:45
  9.2 69.8 %copy-start.1 = (bf16[256,256]{1,0:T(8,128)(2,1)}, bf16[256,256]{1,0:T(8,128)(2,1)S(1)}, u32[]{:S(2)}) copy-start(bf16[256,256]{1,0:T(8,128)(2,1)S(1)} %compare_select_fusion) | copy-start | bytes 393220
  10.1 140.0 %all-reduce.2.cloned.1.call-start = ((), (), s32[]{:S(2)}) async-start(), calls=%async_computation.3 | async-start | bytes 524288 | tf_op jit(solution)/shard_map/psum | solution.py:56
  12.0 139.9 %reduce-scatter.2.cloned.1.call-start = ((), (), s32[]{:S(2)}) async-start(), calls=%async_computation.2 | async-start | bytes 786432 | tf_op jit(solution)/shard_map/reduce_scatter | solution.py:53
Sparse Core Ops, SparseCore 0:
  12.2 63.4 all-gather.1
  99.3 6.6 reduce-scatter.1
Sparse Core Ops, SparseCore 1:
  17.5 132.5 all-reduce.1
where the time goes:
time: 161 us
  waiting for transfers between devices  111 us (69%)
  between operations  15.6 us (10%)
  local copies, waits for them, and re-layouts  13.7 us (9%)
  other arithmetic  12.8 us (8%)
  matrix products  7.62 us (5%)
    all_gather x1, waiting for transfers between devices, body(): lax.all_gather(back_agg, 'graph', axis=0, tiled=True)  60 us
    psum x1, waiting for transfers between devices, body(): weight_grad = lax.psum(partial_weight, ('graph', 'rep'))  51 us
    scatter-add x2, other arithmetic, tile_products(): running.at[local_col[:, slot_index]].add(product * alive[:, None, None])  5.67 us
    gather x2, local copies, waits for them, and re-layouts, tile_products(): chosen = blocks[part_index, local_row[:, slot_index]]  5.41 us
    dot_general x2, matrix products, tile_products(): jnp.einsum('kab,kac->kbc', local_tiles[:, slot_index], chosen, preferred_...  4.91 us
    mul x2, local copies, waits for them, and re-layouts, tile_products(): product * alive[:, None, None]  4.82 us
  transfers between devices with their start and end apart: 3, of which 2 were waited for; matrix products, arithmetic and copies ran while one was open for 19% of the time, Pallas kernels for 0%

commit v1 on v0

--- a/solution.py
+++ b/solution.py
@@ -2,6 +2,18 @@
 import jax.numpy as jnp
 from jax import lax
 from jax.sharding import PartitionSpec as P
+
+
+def collect(array, axis, dim):
+    ways, here = (lax.axis_size(axis), lax.axis_index(axis))
+    grown, reach = (array, 1)
+    while reach < ways:
+        theirs = lax.ppermute(grown, axis, [(d, d ^ reach) for d in range(ways)])
+        mine_first = jnp.concatenate([grown, theirs], axis=dim)
+        theirs_first = jnp.concatenate([theirs, grown], axis=dim)
+        grown = jnp.where(here & reach == 0, mine_first, theirs_first)
+        reach = 2 * reach
+    return grown
 
 
 def tile_products(running, sources, row_count, local_tiles, local_row, local_col, local_count):
@@ -42,7 +54,7 @@
     ).astype(jnp.bfloat16)
     running = tile_products(
         empty,
-        lax.all_gather(back_agg, "graph", axis=0, tiled=True),
+        collect(back_agg, "graph", 0),
         row_count,
         local_tiles,
         local_row,

time: 161 us -> 183 us (1.14)
  waiting for transfers between devices: 111 us -> 126 us
  starting transfers between devices: 0.12 us -> 8.94 us
    ppermute x0 -> x4, waiting for transfers between devices: none -> 62.5 us  [collect(): theirs = lax.ppermute(grown, axis, [(d, d ^ reach) for d in range(ways)])]
    all_gather x1 -> x0, waiting for transfers between devices: 60 us -> none  [body(): lax.all_gather(back_agg, 'graph', axis=0, tiled=True)]
    psum x1, waiting for transfers between devices: 51 us -> 63.4 us  [body(): weight_grad = lax.psum(partial_weight, ('graph', 'rep'))]
    ppermute x0 -> x4, starting transfers between devices: none -> 8.86 us  [collect(): theirs = lax.ppermute(grown, axis, [(d, d ^ reach) for d in range(ways)])]
    select_n x0 -> x4, other arithmetic: none -> 2.63 us  [collect(): grown = jnp.where(here & reach == 0, mine_first, theirs_first)]
    gather x2, local copies, waits for them, and re-layouts: 5.41 us -> 3.21 us  [tile_products(): chosen = blocks[part_index, local_row[:, slot_index]]]
  transfers between devices with their start and end apart: 3 -> 6, of which waited for: 2 -> 5; matrix products, arithmetic and copies ran while one was open for 19% -> 16% of each run, Pallas kernels for 0% -> 0%
where the time goes in v1:
time: 183 us; the launch traced here: 182 us
  waiting for transfers between devices  126 us (69%)
  between operations  15.7 us (9%)
  local copies, waits for them, and re-layouts  12.5 us (7%)
  other arithmetic  11.9 us (7%)
  starting transfers between devices  8.94 us (5%)
  matrix products  7.28 us (4%)
    psum x1, waiting for transfers between devices, body(): weight_grad = lax.psum(partial_weight, ('graph', 'rep'))  63.4 us
    ppermute x4, waiting for transfers between devices, collect(): theirs = lax.ppermute(grown, axis, [(d, d ^ reach) for d in range(ways)])  62.5 us
    ppermute x4, starting transfers between devices, collect(): theirs = lax.ppermute(grown, axis, [(d, d ^ reach) for d in range(ways)])  8.86 us
    dot_general x2, matrix products, tile_products(): jnp.einsum('kab,kac->kbc', local_tiles[:, slot_index], chosen, preferred_...  6.14 us
    scatter-add x2, other arithmetic, tile_products(): running.at[local_col[:, slot_index]].add(product * alive[:, None, None])  5.67 us
    mul x2, local copies, waits for them, and re-layouts, tile_products(): product * alive[:, None, None]  4.82 us
  transfers between devices with their start and end apart: 6, of which 5 were waited for; matrix products, arithmetic and copies ran while one was open for 16% of the time, Pallas kernels for 0%

profile of v1, /device:TPU:0, one launch (start us, length us, event | category | flops | bytes accessed | tf_op | source)
XLA Modules:
  0.0 182.2 jit_solution(8298315513594558520)
XLA Ops:
  8.0 0.0 copy-start
  8.0 0.0 copy-start.4
  8.0 0.0 all-reduce.2.cloned.1.call-start
  8.1 1.0 compare_select_fusion
  9.1 0.0 copy-done
  9.1 0.0 copy-start.2
  9.1 0.2 convolution_convert_fusion
  9.4 3.0 %collective-permute-start = (bf16[256,256]{1,0:T(8,128)(2,1)S(1)}, bf16[256,256]{1,0:T(8,128)(2,1)S(1)}, u32[]{:S(2)}, u32[]{:S(2)}) collective-permute-start(bf16[256,256]{1,0:T(8,128)(2,1)S(1)} %convolution_convert_fusion), channel_id=1, source_target_pairs={{0,2},{2,0},{4,6},{6,4},{8,10},{10,8},{12,14},{14,12},{16,18},{18,... | collective-permute-start | bytes 393224 | tf_op jit(solution)/shard_map/ppermute | solution.py:11
  12.4 3.5 %collective-permute-done = bf16[256,256]{1,0:T(8,128)(2,1)S(1)} collective-permute-done((bf16[256,256]{1,0:T(8,128)(2,1)S(1)}, bf16[256,256]{1,0:T(8,128)(2,1)S(1)}, u32[]{:S(2)}, u32[]{:S(2)}) %collective-permute-start) | collective-permute-done | bytes 131104 | tf_op jit(solution)/shard_map/ppermute | solution.py:11
  15.9 0.1 maximum_select_fusion.3
  16.0 0.0 copy-start.5
  16.0 0.0 copy-start.3
  16.0 1.8 %collective-permute-start.1 = (bf16[512,256]{1,0:T(8,128)(2,1)S(1)}, bf16[512,256]{1,0:T(8,128)(2,1)S(1)}, u32[]{:S(2)}, u32[]{:S(2)}) collective-permute-start(bf16[512,256]{1,0:T(8,128)(2,1)S(1)} %maximum_select_fusion.3), channel_id=1, source_target_pairs={{0,4},{2,6},{4,0},{6,2},{8,12},{10,14},{12,8},{14,10},{16,20},{18,... | collective-permute-start | bytes 786440 | tf_op jit(solution)/shard_map/ppermute | solution.py:11
  17.8 5.7 %collective-permute-done.1 = bf16[512,256]{1,0:T(8,128)(2,1)S(1)} collective-permute-done((bf16[512,256]{1,0:T(8,128)(2,1)S(1)}, bf16[512,256]{1,0:T(8,128)(2,1)S(1)}, u32[]{:S(2)}, u32[]{:S(2)}) %collective-permute-start.1) | collective-permute-done | bytes 262176 | tf_op jit(solution)/shard_map/ppermute | solution.py:11
  23.6 0.2 maximum_select_fusion.2
  23.8 1.6 collective-permute-start.2
  25.4 0.0 copy-done.4
  25.4 0.9 convolution_bitcast_fusion
  26.3 0.0 all-reduce.2.cloned.1.call-update
  26.3 0.0 reduce-scatter.2.cloned.1.call-start
  26.4 0.0 copy-start.8
  26.4 0.0 copy-start.6
  26.4 0.0 copy-start.7
  26.4 9.8 %collective-permute-done.2 = bf16[1024,256]{1,0:T(8,128)(2,1)S(1)} collective-permute-done((bf16[1024,256]{1,0:T(8,128)(2,1)S(1)}, bf16[1024,256]{1,0:T(8,128)(2,1)S(1)}, u32[]{:S(2)}, u32[]{:S(2)}) %collective-permute-start.2) | collective-permute-done | bytes 524320 | tf_op jit(solution)/shard_map/ppermute | solution.py:11
  36.2 0.2 maximum_select_fusion.1
  36.5 0.0 copy-done.2
  36.5 2.5 %collective-permute-start.3 = (bf16[2048,256]{1,0:T(8,128)(2,1)S(1)}, bf16[2048,256]{1,0:T(8,128)(2,1)}, u32[]{:S(2)}, u32[]{:S(2)}) collective-permute-start(bf16[2048,256]{1,0:T(8,128)(2,1)S(1)} %maximum_select_fusion.1), channel_id=1, source_target_pairs={{0,16},{2,18},{4,20},{6,22},{8,24},{10,26},{12,28},{14,30},{16,0},... | collective-permute-start | bytes 3145736 | tf_op jit(solution)/shard_map/ppermute | solution.py:11
  38.9 0.0 copy-done.5
  38.9 0.0 copy-done.3
  38.9 1.0 copy.25
  40.0 0.0 copy-done.8
  40.0 0.0 copy-done.6
  40.0 0.0 copy-done.7
  40.1 43.4 %collective-permute-done.3 = bf16[2048,256]{1,0:T(8,128)(2,1)} collective-permute-done((bf16[2048,256]{1,0:T(8,128)(2,1)S(1)}, bf16[2048,256]{1,0:T(8,128)(2,1)}, u32[]{:S(2)}, u32[]{:S(2)}) %collective-permute-start.3) | collective-permute-done | bytes 1048608 | tf_op jit(solution)/shard_map/ppermute | solution.py:11
  83.5 2.1 %maximum_select_fusion = bf16[4096,256]{1,0:T(8,128)(2,1)S(1)} fusion(bf16[2048,256]{1,0:T(8,128)(2,1)} %collective-permute-done.3, bf16[2048,256]{1,0:T(8,128)(2,1)S(1)} %maximum_select_fusion.1, pred[]{:T(512)S(6)} %eq.12), kind=kLoop, calls=%fused_computation.5 | loop fusion | flops 9437184 | bytes 4194305 | tf_op jit(solution)/shard_map/jit(_where)/select_n | solution.py:14
  85.6 0.0 copy-start.1
  85.6 1.6 gather_fusion.1
  87.2 1.6 gather_fusion
  88.8 0.0 copy-done.1
  88.8 3.1 %multiply_bitcast_fusion = f32[16,128,256]{1,2,0:T(8,128)} fusion(bf16[16,128,256]{2,1,0:T(8,128)(2,1)} %gather_fusion.1, f32[16]{0:T(128)S(1)} %get-tuple-element.13, bf16[16,2,128,128]{3,2,0,1:T(8,128)(2,1)S(1)} %bitcast.44), kind=kOutput, calls=%fused_computation.6 | convolution fusion | flops 134742016 | bytes 3670528 | tf_op jit(solution)/shard_map/kab,kac->kbc/dot_general | solution.py:27
  91.9 1.9 %copy.20 = f32[16,128,256]{2,1,0:T(8,128)S(1)} copy(f32[16,128,256]{1,2,0:T(8,128)} %multiply_bitcast_fusion) | data formatting | bytes 4194304 | tf_op jit(solution)/shard_map/mul | solution.py:31
  93.8 3.1 %multiply_bitcast_fusion.1 = f32[16,128,256]{1,2,0:T(8,128)} fusion(bf16[16,128,256]{2,1,0:T(8,128)(2,1)} %gather_fusion, f32[16]{0:T(128)S(1)} %get-tuple-element.14, bf16[16,2,128,128]{3,2,0,1:T(8,128)(2,1)S(1)} %bitcast.45), kind=kOutput, calls=%fused_computation.7 | convolution fusion | flops 134742016 | bytes 3670528 | tf_op jit(solution)/shard_map/kab,kac->kbc/dot_general | solution.py:27
  96.9 2.9 %copy.18 = f32[16,128,256]{2,1,0:T(8,128)} copy(f32[16,128,256]{1,2,0:T(8,128)} %multiply_bitcast_fusion.1) | data formatting | bytes 4194304 | tf_op jit(solution)/shard_map/mul | solution.py:31
  99.8 3.5 %scatter_fusion = f32[4,128,256]{2,1,0:T(8,128)S(1)} fusion(f32[4,128,256]{2,1,0:T(8,128)S(1)} %broadcast_in_dim.10, s32[16]{0:T(128)S(1)} %get-tuple-element.12, f32[16,128,256]{2,1,0:T(8,128)} %copy.18), kind=kCustom, calls=%fused_computation.3 | custom fusion | flops 524288 | bytes 6291520 | tf_op jit(solution)/shard_map/scatter-add | solution.py:31
  103.3 2.2 %scatter_fusion.1 = f32[4,128,256]{2,1,0:T(8,128)S(1)} fusion(f32[4,128,256]{2,1,0:T(8,128)S(1)} %scatter_fusion, s32[16]{0:T(128)S(1)} %get-tuple-element.11, f32[16,128,256]{2,1,0:T(8,128)S(1)} %copy.20), kind=kCustom, calls=%fused_computation.4 | custom fusion | flops 524288 | bytes 6291520 | tf_op jit(solution)/shard_map/scatter-add | solution.py:31
  105.5 1.6 gather_fusion.2
  107.1 0.9 broadcast_select_fusion
  108.0 0.0 reduce-scatter.2.cloned.1.call-update
  108.0 63.4 %all-reduce.2.cloned.1.call-done = f32[256,256]{0,1:T(8,128)} async-done(((f32[256,256]{0,1:T(8,128)}), f32[256,256]{0,1:T(8,128)}) %all-reduce.2.cloned.1.call-update) | async-done | bytes 262160 | tf_op jit(solution)/shard_map/psum | solution.py:68
  171.4 1.8 copy.21
  173.2 0.0 reduce-scatter.2.cloned.1.call-done
  173.2 1.6 convert_element_type.31
  (7 shorter events, 0.1 us)
Async XLA Ops:
  8.0 1.1 copy-start
  8.0 17.3 %copy-start.4 = (bf16[256,256]{1,0:T(8,128)(2,1)S(1)}, bf16[256,256]{1,0:T(8,128)(2,1)}, u32[]{:S(2)}) copy-start(bf16[256,256]{1,0:T(8,128)(2,1)} %param.11) | copy-start | bytes 393220
  8.0 163.4 %all-reduce.2.cloned.1.call-start = ((), (), s32[]{:S(2)}) async-start(), calls=%async_computation.2 | async-start | bytes 524288 | tf_op jit(solution)/shard_map/psum | solution.py:68
  9.1 27.3 %copy-start.2 = (bf16[256,256]{1,0:T(8,128)(2,1)}, bf16[256,256]{1,0:T(8,128)(2,1)S(1)}, u32[]{:S(2)}) copy-start(bf16[256,256]{1,0:T(8,128)(2,1)S(1)} %compare_select_fusion) | copy-start | bytes 393220
  9.4 6.5 %collective-permute-start = (bf16[256,256]{1,0:T(8,128)(2,1)S(1)}, bf16[256,256]{1,0:T(8,128)(2,1)S(1)}, u32[]{:S(2)}, u32[]{:S(2)}) collective-permute-start(bf16[256,256]{1,0:T(8,128)(2,1)S(1)} %convolution_convert_fusion), channel_id=1, source_target_pairs={{0,2},{2,0},{4,6},{6,4},{8,10},{10,8},{12,14},{14,12},{16,18},{18,... | collective-permute-start | bytes 393224 | tf_op jit(solution)/shard_map/ppermute | solution.py:11
  16.0 23.0 %copy-start.5 = (s32[1,512]{1,0:T(1,128)S(1)}, s32[1,512]{1,0:T(1,128)}, u32[]{:S(2)}) copy-start(s32[1,512]{1,0:T(1,128)} %param.17) | copy-start | bytes 6148
  16.0 23.0 %copy-start.3 = (bf16[1,1,16,2,128,128]{5,4,3,2,1,0:T(8,128)(2,1)S(1)}, bf16[1,1,16,2,128,128]{5,4,3,2,1,0:T(8,128)(2,1)}, u32[]{:S(2)}) copy-start(bf16[1,1,16,2,128,128]{5,4,3,2,1,0:T(8,128)(2,1)} %param.13) | copy-start | bytes 3145732
  16.0 7.6 %collective-permute-start.1 = (bf16[512,256]{1,0:T(8,128)(2,1)S(1)}, bf16[512,256]{1,0:T(8,128)(2,1)S(1)}, u32[]{:S(2)}, u32[]{:S(2)}) collective-permute-start(bf16[512,256]{1,0:T(8,128)(2,1)S(1)} %maximum_select_fusion.3), channel_id=1, source_target_pairs={{0,4},{2,6},{4,0},{6,2},{8,12},{10,14},{12,8},{14,10},{16,20},{18,... | collective-permute-start | bytes 786440 | tf_op jit(solution)/shard_map/ppermute | solution.py:11
  23.8 12.4 %collective-permute-start.2 = (bf16[1024,256]{1,0:T(8,128)(2,1)S(1)}, bf16[1024,256]{1,0:T(8,128)(2,1)S(1)}, u32[]{:S(2)}, u32[]{:S(2)}) collective-permute-start(bf16[1024,256]{1,0:T(8,128)(2,1)S(1)} %maximum_select_fusion.2), channel_id=1, source_target_pairs={{0,8},{2,10},{4,12},{6,14},{8,0},{10,2},{12,4},{14,6},{16,24},{18,... | collective-permute-start | bytes 1572872 | tf_op jit(solution)/shard_map/ppermute | solution.py:11
  26.3 146.9 %reduce-scatter.2.cloned.1.call-start = ((), (), s32[]{:S(2)}) async-start(), calls=%async_computation.1 | async-start | bytes 786432 | tf_op jit(solution)/shard_map/reduce_scatter | solution.py:65
  26.4 13.6 %copy-start.8 = (s32[1,1,16]{2,1,0:T(1,128)S(1)}, s32[1,1,16]{2,1,0:T(1,128)}, u32[]{:S(2)}) copy-start(s32[1,1,16]{2,1,0:T(1,128)} %param.16) | copy-start | bytes 196
  26.4 13.6 %copy-start.6 = (s32[1,1,16,2]{2,3,1,0:T(2,128)S(1)}, s32[1,1,16,2]{2,3,1,0:T(2,128)}, u32[]{:S(2)}) copy-start(s32[1,1,16,2]{2,3,1,0:T(2,128)} %param.14) | copy-start | bytes 388
  26.4 13.6 %copy-start.7 = (s32[1,1,16,2]{2,3,1,0:T(2,128)S(1)}, s32[1,1,16,2]{2,3,1,0:T(2,128)}, u32[]{:S(2)}) copy-start(s32[1,1,16,2]{2,3,1,0:T(2,128)} %param.15) | copy-start | bytes 388
  36.5 47.1 %collective-permute-start.3 = (bf16[2048,256]{1,0:T(8,128)(2,1)S(1)}, bf16[2048,256]{1,0:T(8,128)(2,1)}, u32[]{:S(2)}, u32[]{:S(2)}) collective-permute-start(bf16[2048,256]{1,0:T(8,128)(2,1)S(1)} %maximum_select_fusion.1), channel_id=1, source_target_pairs={{0,16},{2,18},{4,20},{6,22},{8,24},{10,26},{12,28},{14,30},{16,0},... | collective-permute-start | bytes 3145736 | tf_op jit(solution)/shard_map/ppermute | solution.py:11
  85.6 3.2 %copy-start.1 = (bf16[1,1,16,2,128,128]{5,4,2,3,1,0:T(8,128)(2,1)S(1)}, bf16[1,1,16,2,128,128]{5,4,2,3,1,0:T(8,128)(2,1)}, u32[]{:S(2)}) copy-start(bf16[1,1,16,2,128,128]{5,4,2,3,1,0:T(8,128)(2,1)} %copy.25) | copy-start | bytes 3145732
Sparse Core Ops, SparseCore 0:
  26.4 144.9 all-reduce.1
Sparse Core Ops, SparseCore 1:
  108.1 8.3 reduce-scatter.1
